TPU v7x, 256 devices: a whole 4x4x8 slice. The times are simulated.
256 devices in a mesh: grp: 16 (over z, core), blk: 16 (over x, y).
Axes of the slice: x: 4, y: 4, z: 8, core: 2. Of those that a mesh axis runs over, the one named last changes fastest.
Arguments:
- block_tiles: bfloat16 [512, 32, 256, 256], P(('grp', 'blk')), may hold values from -0.0625 to 0.0625
- col_blocks: int32 [512, 32], P(('grp', 'blk')), may hold values from 0 to 511, as said below
- scales: float32 [512, 32], P(('grp', 'blk')), may hold values from 0.5 to 2
- x_start: float32 [32, 131072], P(None, ('grp', 'blk')), may hold values from -6 to 6
- p_start: float32 [32, 131072], P(None, ('grp', 'blk')), may hold values from -6 to 6
Outputs:
- x_next: float32 [32, 131072], P(None, ('grp', 'blk'))
- p_next: float32 [32, 131072], P(None, ('grp', 'blk'))
Inputs may be any that keep to these rules, and one draw needn't show every extreme that they name: col_blocks[b, 0] = b. With g = b // 32: entries 1 to 23 of row b lie in block rows g * 32 to (g + 1) * 32 - 1; entries 3 * 8 to 27 lie in the block rows of cluster (g - 1) modulo 16; entries 7 * 4 to 31 lie in those of cluster (g + 1) modulo 16.
All inputs are finite; a program needn't handle non-finite values.
Results may differ from a plain program's by a relative error of at most 0.003.
Values may be sent and summed in bfloat16 or wider, within the bound.
A program may use at most 64 MiB of HBM per device.

v0:
```python
import jax
import jax.numpy as jnp
from jax import lax
from jax.sharding import PartitionSpec as P

NS_STEPS = 8


def passed_along(shard, axis, by):
    size = lax.axis_size(axis)
    return lax.ppermute(shard, axis, [(i, (i + by) % size) for i in range(size)])


def lower_solve(factor, rhs, transposed=False):
    return lax.linalg.triangular_solve(
        factor, rhs, left_side=True, lower=True, transpose_a=transposed
    )


def fetch_picked(rounded, col_blocks, tile_width):
    width_rows = rounded.shape[0]
    block_rows = col_blocks.shape[0]
    slot_count = col_blocks.shape[1]
    own_panel = lax.all_gather(rounded, "blk", axis=1, tiled=True)
    prev_panel = passed_along(own_panel, "grp", 1)
    next_panel = passed_along(own_panel, "grp", -1)
    stacked = jnp.concatenate([prev_panel, own_panel, next_panel], axis=1)
    group_blocks = stacked.shape[1] // (3 * tile_width)
    groups = lax.axis_size("grp")
    group_index = lax.axis_index("grp")
    blocks = stacked.reshape(width_rows, 3 * group_blocks, tile_width)
    relative = (col_blocks // group_blocks - group_index) % groups
    local_index = (relative + 1) % groups * group_blocks + col_blocks % group_blocks
    picked = jnp.take(blocks, local_index.reshape(-1), axis=1)
    return picked.reshape(width_rows, block_rows, slot_count, tile_width)


def apply_local(field, block_tiles, col_blocks, scales):
    width_rows = field.shape[0]
    tile_width = block_tiles.shape[2]
    picked = fetch_picked(field.astype(jnp.bfloat16), col_blocks, tile_width)
    products = lax.dot_general(
        picked, block_tiles, (((3,), (3,)), ((1, 2), (0, 1))), preferred_element_type=jnp.float32
    )
    mixture = jnp.einsum("bjwr,bj->wbr", products, scales, precision=lax.Precision.HIGHEST)
    return field - mixture.reshape(width_rows, -1)


def spectral_filter(ritz_matrix):
    order_size = ritz_matrix.shape[0]
    identity = jnp.eye(order_size, dtype=jnp.float32)
    spectral_shift = jnp.trace(ritz_matrix) / order_size
    centred = spectral_shift * identity - ritz_matrix
    iterate = centred / jnp.sqrt(jnp.sum(centred * centred) + 1e-06)
    for repeat in range(NS_STEPS):
        cubed = jnp.dot(
            iterate,
            jnp.dot(iterate, iterate, precision=lax.Precision.HIGHEST),
            precision=lax.Precision.HIGHEST,
        )
        iterate = 1.5 * iterate - 0.5 * cubed
    return 0.5 * (identity + iterate)


def per_device(block_tiles, col_blocks, scales, x_start, p_start):
    high = lax.Precision.HIGHEST
    vectors = x_start.shape[0]
    item_count = x_start.shape[1] * lax.axis_size("grp") * lax.axis_size("blk")
    both_images = apply_local(
        jnp.concatenate([x_start, p_start], axis=0), block_tiles, col_blocks, scales
    )
    image_x = both_images[:vectors]
    image_p = both_images[vectors:]
    gram_x, cross_x = lax.psum(
        (jnp.dot(x_start, x_start.T, precision=high), jnp.dot(x_start, image_x.T, precision=high)),
        ("grp", "blk"),
    )
    gram_x = gram_x / item_count
    cross_x = cross_x / item_count
    chol_x = jnp.linalg.cholesky(gram_x)
    coupling = lower_solve(chol_x, lower_solve(chol_x, cross_x), True)
    residual = image_x - jnp.dot(coupling.T, x_start, precision=high)
    image_r = apply_local(residual, block_tiles, col_blocks, scales)
    full_basis = jnp.concatenate([x_start, residual, p_start], axis=0)
    images = jnp.concatenate([image_x, image_r, image_p], axis=0)
    gram_basis, projected = lax.psum(
        (
            jnp.dot(full_basis, full_basis.T, precision=high),
            jnp.dot(full_basis, images.T, precision=high),
        ),
        ("grp", "blk"),
    )
    gram_basis = gram_basis / item_count
    projected = projected / item_count
    chol_lower = jnp.linalg.cholesky(gram_basis)
    half_solved = lower_solve(chol_lower, projected)
    ritz_matrix = lower_solve(chol_lower, half_solved.T)
    ritz_matrix = 0.5 * (ritz_matrix + ritz_matrix.T)
    filtered = spectral_filter(ritz_matrix)
    coefficients = lower_solve(chol_lower, filtered[:, :vectors], True)
    new_x = jnp.dot(coefficients.T, full_basis, precision=high)
    new_p = jnp.dot(coefficients[vectors:].T, full_basis[vectors:], precision=high)
    gram_new = lax.psum(jnp.dot(new_x, new_x.T, precision=high), ("grp", "blk")) / item_count
    chol_new = jnp.linalg.cholesky(gram_new)
    x_next = lower_solve(chol_new, new_x)
    p_next = lower_solve(chol_new, new_p)
    return (x_next, p_next)


def solution(mesh):
    placed = (
        P(("grp", "blk"), None, None, None),
        P(("grp", "blk"), None),
        P(("grp", "blk"), None),
        P(None, ("grp", "blk")),
        P(None, ("grp", "blk")),
    )
    return jax.shard_map(
        per_device,
        mesh=mesh,
        in_specs=placed,
        out_specs=(P(None, ("grp", "blk")), P(None, ("grp", "blk"))),
        check_vma=False,
    )
```

profile of v0, /device:TPU:1, one launch (start us, length us, event | category | flops | bytes accessed | tf_op | source)
XLA Modules:
  0.0 578.3 jit_solution(16436396034150240945)
XLA Ops:
  9.6 52.2 %all-gather.2.cloned.1.call-done = bf16[64,8192]{1,0:T(8,128)(2,1)} async-done(((bf16[64,512]{1,0:T(8,128)(2,1)}), bf16[64,8192]{1,0:T(8,128)(2,1)}) %all-gather.2.cloned.1.call-update) | async-done | bytes 1048592 | tf_op jit(solution)/shard_map/all_gather | solution.py:24
  61.8 3.2 collective-permute-start
  66.9 10.1 %collective-permute-done = bf16[64,8192]{1,0:T(8,128)(2,1)S(1)} collective-permute-done((bf16[64,8192]{1,0:T(8,128)(2,1)}, bf16[64,8192]{1,0:T(8,128)(2,1)S(1)}, u32[]{:S(2)}, u32[]{:S(2)}) %collective-permute-start) | collective-permute-done | bytes 1048608 | tf_op jit(solution)/shard_map/ppermute | solution.py:11
  77.1 2.4 collective-permute-done.1
  79.4 1.3 pad_maximum_fusion
  81.2 2.0 gather_fusion
  83.2 6.7 %fusion.4 = f32[2,32,64,256]{3,2,1,0:T(8,128)S(1)} fusion(bf16[2,32,256,256]{3,2,1,0:T(8,128)(2,1)} %param.10, bf16[64,2,32,256]{3,0,2,1:T(8,128)(2,1)} %bitcast.128, pred[2,32]{1,0:T(4,128)(4,1)S(1)} %get-tuple-element.11), kind=kOutput, calls=%fused_computation.8 | convolution fusion | flops 537919488 | bytes 14680128 | tf_op jit(solution)/shard_map/dot_general | solution.py:42
  89.9 4.6 fusion
  94.9 77.5 %all-reduce.1 = (f32[32,32]{0,1:T(8,128)S(1)}, f32[32,32]{0,1:T(8,128)S(1)}) all-reduce(f32[32,32]{0,1:T(8,128)S(1)} %fusion.93, f32[32,32]{0,1:T(8,128)S(1)} %convolution_bitcast_fusion.1), channel_id=1, replica_groups=mesh['grp'=16,'blk'=16] {'grp','blk'}, use_global_device_ids=true, to_apply=%region_0.1 | all-reduce | flops 2048 | bytes 16384 | tf_op jit(solution)/shard_map/psum | solution.py:74
  172.5 2.9 cholesky.85
  176.7 2.4 custom-call.19
  179.8 18.1 %all_gather.7 = bf16[32,8192]{1,0:T(8,128)(2,1)S(1)} all-gather(bf16[32,512]{1,0:T(8,128)(2,1)S(1)} %get-tuple-element.15), channel_id=1, replica_groups=mesh['grp'=16,'blk'=16] {'blk'}, dimensions={1}, use_global_device_ids=true | all-gather | bytes 557056 | tf_op jit(solution)/shard_map/all_gather | solution.py:24
  197.9 4.6 collective-permute-start.2
  202.5 1.7 collective-permute-start.3
  205.1 3.5 collective-permute-done.2
  208.6 2.8 collective-permute-done.3
  212.3 5.9 %fusion.14 = f32[2,32,32,256]{3,2,1,0:T(8,128)S(1)} fusion(bf16[2,32,256,256]{3,2,1,0:T(8,128)(2,1)} %param.10, bf16[32,2,32,256]{3,0,2,1:T(8,128)(2,1)S(1)} %bitcast.131, pred[2,32]{1,0:T(4,128)(4,1)S(1)} %get-tuple-element.11), kind=kOutput, calls=%fused_computation.30 | convolution fusion | flops 268959744 | bytes 11534400 | tf_op jit(solution)/shard_map/dot_general | solution.py:42
  218.2 2.4 fusion.2
  221.7 239.7 %all-reduce.4.cloned.1.call-done = (f32[96,96]{0,1:T(8,128)}, f32[96,96]{0,1:T(8,128)}) async-done(((f32[96,96]{0,1:T(8,128)}, f32[96,96]{0,1:T(8,128)}), (f32[96,96]{0,1:T(8,128)}, f32[96,96]{0,1:T(8,128)})) %all-reduce.4.cloned.1.call-update) | async-done | bytes 73744 | tf_op jit(solution)/shard_map/psum | solution.py:86
  463.1 8.8 %cholesky.44 = f32[96,96]{1,0:T(8,128)S(1)} custom-call(f32[96,96]{1,0:T(8,128)S(1)} %fusion.42), custom_call_target="Cholesky" | custom-call | tf_op jit(solution)/shard_map/jit(cholesky)/cholesky | solution.py:95
  473.2 7.4 %custom-call.20 = f32[1,96,96]{1,2,0:T(8,128)S(1)} custom-call(f32[1,96,96]{2,1,0:T(8,128)S(1)} %fusion.31), custom_call_target="InvertDiagBlocksLowerTriangular" | custom-call | tf_op jit(solution)/shard_map/triangular_solve | solution.py:15
  488.6 74.3 %psum.39 = f32[32,32]{0,1:T(8,128)S(1)} all-reduce(f32[32,32]{0,1:T(8,128)S(1)} %fusion.102), channel_id=1, replica_groups=mesh['grp'=16,'blk'=16] {'grp','blk'}, use_global_device_ids=true, to_apply=%region_10.13 | all-reduce | flops 1024 | bytes 8192 | tf_op jit(solution)/shard_map/psum | solution.py:103
  563.0 2.9 cholesky.96
  567.3 2.4 custom-call.25
  (82 shorter events, 22.9 us)
Async XLA Ops:
  7.2 82.7 %copy-start = (f32[2,32]{1,0:T(2,128)S(1)}, f32[2,32]{1,0:T(2,128)}, u32[]{:S(2)}) copy-start(f32[2,32]{1,0:T(2,128)} %param.12) | copy-start | bytes 772
  7.2 54.6 %all-gather.2.cloned.1.call-start = ((), (), s32[]{:S(2)}) async-start(), calls=%async_computation | async-start | bytes 1114112 | tf_op jit(solution)/shard_map/all_gather | solution.py:24
  9.6 451.8 %all-reduce.4.cloned.1.call-start = ((), (), s32[]{:S(2)}) async-start(), calls=%async_computation.1 | async-start | bytes 196608 | tf_op jit(solution)/shard_map/psum | solution.py:86
  61.8 15.3 %collective-permute-start = (bf16[64,8192]{1,0:T(8,128)(2,1)}, bf16[64,8192]{1,0:T(8,128)(2,1)S(1)}, u32[]{:S(2)}, u32[]{:S(2)}) collective-permute-start(bf16[64,8192]{1,0:T(8,128)(2,1)} %all-gather.2.cloned.1.call-done), channel_id=1, source_target_pairs={{0,16},{16,32},{32,48},{48,64},{64,80},{80,96},{96,112},{112,128},... | collective-permute-start | bytes 3145736 | tf_op jit(solution)/shard_map/ppermute | solution.py:11
  65.0 14.4 %collective-permute-start.1 = (bf16[64,8192]{1,0:T(8,128)(2,1)}, bf16[64,8192]{1,0:T(8,128)(2,1)S(1)}, u32[]{:S(2)}, u32[]{:S(2)}) collective-permute-start(bf16[64,8192]{1,0:T(8,128)(2,1)} %all-gather.2.cloned.1.call-done), channel_id=1, source_target_pairs={{0,240},{16,0},{32,16},{48,32},{64,48},{80,64},{96,80},{112,96},{1... | collective-permute-start | bytes 3145736 | tf_op jit(solution)/shard_map/ppermute | solution.py:11
  89.9 4.8 copy-start.1
  89.9 114.2 %copy-start.2 = (f32[32,512]{1,0:T(8,128)S(1)}, f32[32,512]{1,0:T(8,128)}, u32[]{:S(2)}) copy-start(f32[32,512]{1,0:T(8,128)} %param.14) | copy-start | bytes 196612
  197.9 10.7 %collective-permute-start.2 = (bf16[32,8192]{1,0:T(8,128)(2,1)S(1)}, bf16[32,8192]{1,0:T(8,128)(2,1)S(1)}, u32[]{:S(2)}, u32[]{:S(2)}) collective-permute-start(bf16[32,8192]{1,0:T(8,128)(2,1)S(1)} %all_gather.7), channel_id=1, source_target_pairs={{0,16},{16,32},{32,48},{48,64},{64,80},{80,96},{96,112},{112,128},... | collective-permute-start | bytes 1572872 | tf_op jit(solution)/shard_map/ppermute | solution.py:11
  202.5 8.9 %collective-permute-start.3 = (bf16[32,8192]{1,0:T(8,128)(2,1)S(1)}, bf16[32,8192]{1,0:T(8,128)(2,1)S(1)}, u32[]{:S(2)}, u32[]{:S(2)}) collective-permute-start(bf16[32,8192]{1,0:T(8,128)(2,1)S(1)} %all_gather.7), channel_id=1, source_target_pairs={{0,240},{16,0},{32,16},{48,32},{64,48},{80,64},{96,80},{112,96},{1... | collective-permute-start | bytes 1572872 | tf_op jit(solution)/shard_map/ppermute | solution.py:11
Sparse Core Ops, SparseCore 0:
  11.0 50.7 all-gather.1
  221.8 239.5 all-reduce.3
where the time goes:
time: 579 us; the launch traced here: 578 us
  waiting for transfers between devices  311 us (54%)
  blocking collectives  170 us (29%)
  other arithmetic  36.5 us (6%)
  matrix products  30.4 us (5%)
  between operations  15.7 us (3%)
  starting transfers between devices  9.49 us (2%)
    psum x1, waiting for transfers between devices, per_device(): lax.psum((jnp.dot(full_basis, full_basis.T, precision=high), jnp.dot(full...  240 us
    psum x1, blocking collectives, per_device(): lax.psum((jnp.dot(x_start, x_start.T, precision=high), jnp.dot(x_start, i...  77.5 us
    psum x1, blocking collectives, per_device(): lax.psum(jnp.dot(new_x, new_x.T, precision=high), ('grp', 'blk'))  74.3 us
    all_gather x1, waiting for transfers between devices, fetch_picked(): own_panel = lax.all_gather(rounded, 'blk', axis=1, tiled=True)  52.2 us
    ppermute x4, waiting for transfers between devices, passed_along(): lax.ppermute(shard, axis, [(i, (i + by) % size) for i in range(size)])  18.8 us
    all_gather x1, blocking collectives, fetch_picked(): own_panel = lax.all_gather(rounded, 'blk', axis=1, tiled=True)  18.1 us
    another operation x6, other arithmetic, lower_solve(): lax.linalg.triangular_solve(factor, rhs, left_side=True, lower=True, tran...  14.2 us
    dot_general x2, matrix products, apply_local(): lax.dot_general(picked, block_tiles, (((3,), (3,)), ((1, 2), (0, 1))), pr...  12.6 us
  transfers between devices with their start and end apart: 6, of which 6 were waited for; matrix products, arithmetic and copies ran while one was open for 0% of the time, Pallas kernels for 0%

commit v1 on v0

v1 whole, which is shorter than its diff:
```python
import functools

import jax
import jax.numpy as jnp
from jax import lax
from jax.experimental import pallas as pl
from jax.experimental.pallas import tpu as pltpu
from jax.sharding import PartitionSpec as P

NS_STEPS = 8
PANEL = 8
HIGH = lax.Precision.HIGHEST
F32 = jnp.float32
BF16 = jnp.bfloat16


def dot_nt(a, b, precision=None):
    return lax.dot_general(
        a, b, (((1,), (1,)), ((), ())), precision=precision, preferred_element_type=F32
    )


def dot_nn(a, b, precision=HIGH):
    return jnp.dot(a, b, precision=precision, preferred_element_type=F32)


def collect(
    n_grp,
    n_blk,
    side,
    cols_hbm,
    scales_hbm,
    x_hbm,
    p_hbm,
    tiles_hbm,
    gram_ref,
    image_ref,
    s_ref,
    cols,
    scales,
    x_ref,
    p_ref,
    tiles,
    x_panel,
    p_panel,
    s_panel,
    want_next,
    want_prev,
    x_out,
    x_in,
    p_out,
    p_in,
    s_out,
    s_in,
    partial,
    rs_buf,
    ar_buf,
    mine_t,
    mate_t,
    blk_t,
    z_t,
    load_sem,
    ask_send,
    ask_recv,
    x_send,
    x_recv,
    p_send,
    p_recv,
    p_send2,
    p_recv2,
    s_send,
    s_recv,
    z_send,
    z_recv,
    rs_send,
    rs_recv,
    ar_send,
    ar_recv,
    ag_send,
    ag_recv,
    mate_send,
    mate_recv,
    blk_send,
    blk_recv,
    zt_send,
    zt_recv,
):
    me_g = lax.axis_index("grp")
    me_b = lax.axis_index("blk")
    me_x, me_y = me_b // side, lax.rem(me_b, side)
    nxt = lax.rem(me_g + 1, n_grp)
    prv = lax.rem(me_g + n_grp - 1, n_grp)
    core = lax.rem(me_g, 2)
    mate = me_g + 1 - 2 * core
    rows_here, slots = cols.shape
    k = x_ref.shape[0]
    width = tiles.shape[2]
    cluster = n_blk * rows_here
    inner = 3 * slots // 4
    outer = slots // 8
    n_early = 3 * k // 8
    half = k // 2

    def load(src, dst, i):
        return pltpu.make_async_copy(src, dst, load_sem.at[i])

    load_x, load_p = load(x_hbm, x_ref, 0), load(p_hbm, p_ref, 1)
    load_small = [load(cols_hbm, cols, 2), load(scales_hbm, scales, 3)]
    load_tiles = [load(tiles_hbm.at[i], tiles.at[i], 4 + i) for i in range(rows_here)]
    for copy in [load_x, load_p, *load_small, *load_tiles]:
        copy.start()

    barrier = pltpu.get_barrier_semaphore()

    def greet(grp, blk):
        pl.semaphore_signal(
            barrier, inc=1, device_id=(grp, blk), device_id_type=pl.DeviceIdType.MESH
        )

    def greet_blk(d, c):
        greet(me_g, lax.rem(me_b + d, n_blk))
        return c

    def greet_grp(d, c):
        greet(lax.rem(me_g + d, n_grp), me_b)
        return c

    lax.fori_loop(1, n_blk, greet_blk, 0)
    lax.fori_loop(1, n_grp, greet_grp, 0)

    def block(ref, i):
        return ref[:, i * width : (i + 1) * width].astype(BF16)

    load_x.wait()
    for i in range(rows_here):
        x_panel[i, me_x, me_y] = block(x_ref, i)
    load_p.wait()
    for i in range(rows_here):
        p_panel[i, me_x, me_y] = block(p_ref, i)
    for copy in load_small:
        copy.wait()
    pl.semaphore_wait(barrier, n_blk - 1 + n_grp - 1)

    def remote(src, dst, send, recv, grp, blk):
        return pltpu.make_async_remote_copy(
            src_ref=src,
            dst_ref=dst,
            send_sem=send,
            recv_sem=recv,
            device_id=(grp, blk),
            device_id_type=pl.DeviceIdType.MESH,
        )

    ask = [
        remote(cols, want_next, ask_send.at[0], ask_recv.at[0], prv, me_b),
        remote(cols, want_prev, ask_send.at[1], ask_recv.at[1], nxt, me_b),
    ]

    def each(count, act):
        def body(d, c):
            act(d)
            return c

        lax.fori_loop(1, count, body, 0)

    def along_x(d):
        return lax.rem(me_x + d, side) * side + me_y

    def along_y(d):
        return me_x * side + lax.rem(me_y + d, side)

    def p_first(d):
        a, b = p_panel.at[0, me_x, me_y], p_panel.at[1, me_x, me_y]
        return [
            remote(a, a, p_send.at[0, d], p_recv.at[0, d], me_g, along_x(d)),
            remote(b, b, p_send.at[1, d], p_recv.at[1, d], me_g, along_y(d)),
        ]

    def p_second(d):
        a, b = p_panel.at[0, :, me_y], p_panel.at[1, me_x]
        return [
            remote(a, a, p_send2.at[0, d], p_recv2.at[0, d], me_g, along_y(d)),
            remote(b, b, p_send2.at[1, d], p_recv2.at[1, d], me_g, along_x(d)),
        ]

    def near(buf, send, recv, d):
        a, b = buf.at[0, me_x, me_y], buf.at[1, me_x, me_y]
        return [
            remote(a, a, send.at[0, side, d], recv.at[0, side, d], me_g, along_x(d)),
            remote(b, b, send.at[1, side, d], recv.at[1, side, d], me_g, along_y(d)),
        ]

    def onward(buf, send, recv, e, d):
        from_x, from_y = lax.rem(me_x + side - e, side), lax.rem(me_y + side - e, side)
        a, b = buf.at[0, from_x, me_y], buf.at[1, me_x, from_y]
        return [
            remote(a, a, send.at[0, e, d], recv.at[0, e, d], me_g, along_y(d)),
            remote(b, b, send.at[1, e, d], recv.at[1, e, d], me_g, along_x(d)),
        ]

    def start(copies):
        for copy in copies:
            copy.start()

    def wait(copies):
        for copy in copies:
            copy.wait()

    def send_own(buf, send, recv):
        each(side, lambda d: start(near(buf, send, recv, d)))
        each(side, lambda d: start(onward(buf, send, recv, 0, d)))

    def pass_on(buf, send, recv):
        def arrived(e):
            for copy in near(buf, send, recv, e):
                copy.wait_recv()
            each(side, lambda d: start(onward(buf, send, recv, e, d)))

        each(side, arrived)

    def all_in(buf, send, recv):
        def sent(d):
            for copy in near(buf, send, recv, d):
                copy.wait_send()
            wait(onward(buf, send, recv, 0, d))

        each(side, sent)
        each(side, lambda e: each(side, lambda d: wait(onward(buf, send, recv, e, d))))

    def crossed(buf):
        def get(c):
            c = lax.rem(c, cluster)
            at = c // rows_here
            return buf[lax.rem(c, rows_here), at // side, lax.rem(at, side)]

        return get

    def exchange(out, into, at):
        return [
            remote(out.at[0], into.at[0], z_send.at[at], z_recv.at[at], nxt, me_b),
            remote(out.at[1], into.at[1], z_send.at[at + 1], z_recv.at[at + 1], prv, me_b),
        ]

    def pick(get, out):
        for i in range(rows_here):
            for j in range(outer):
                out[0, i * outer + j] = get(want_next[i, inner + j])
                out[1, i * outer + j] = get(want_prev[i, inner + outer + j])

    def mix_inner(get):
        sums = []
        for i in range(rows_here):

            def body(j, acc, i=i):
                return acc + dot_nt(get(cols[i, j]), tiles[i, j]) * scales[i, j]

            sums.append(lax.fori_loop(0, inner, body, jnp.zeros((k, width), F32), unroll=8))
        return sums

    def mix_outer(sums, into):
        for i in range(rows_here):
            for j in range(outer):
                a, b = inner + j, inner + outer + j
                sums[i] += dot_nt(into[0, i * outer + j], tiles[i, a]) * scales[i, a]
                sums[i] += dot_nt(into[1, i * outer + j], tiles[i, b]) * scales[i, b]
        return sums

    for copy in ask:
        copy.start()
    send_own(x_panel, x_send, x_recv)
    pass_on(x_panel, x_send, x_recv)
    for copy in ask:
        copy.wait()
    all_in(x_panel, x_send, x_recv)
    pick(crossed(x_panel), x_out)
    x_across = exchange(x_out, x_in, 0)
    for copy in x_across:
        copy.start()
    for d in range(1, side):
        for copy in p_first(d):
            copy.start()
    for copy in load_tiles:
        copy.wait()
    sums = mix_inner(crossed(x_panel))
    for d in range(1, side):
        for copy in p_first(d):
            copy.wait()
    for d in range(1, side):
        for copy in p_second(d):
            copy.start()
    for copy in x_across:
        copy.wait()
    sums = mix_outer(sums, x_in)
    for i in range(rows_here):
        s_panel[i, me_x, me_y] = sums[i].astype(BF16)
        s_ref[:, i * width : (i + 1) * width] = sums[i]
    send_own(s_panel, s_send, s_recv)

    basis = jnp.concatenate([x_ref[...], s_ref[...], p_ref[...]], axis=0)
    partial[0 : 3 * k, 0 : 3 * k] = dot_nt(basis, basis, HIGH)
    partial[0 : 3 * k, 3 * k :] = jnp.zeros((3 * k, k), F32)
    partial[3 * k :, 3 * k :] = jnp.zeros((k, k), F32)

    def chunk_out(d):
        to = lax.rem(me_b + d, n_blk)
        src = partial.at[pl.ds(pl.multiple_of(to * 8, 8), 8)]
        return to, remote(src, rs_buf.at[me_b], rs_send.at[d], rs_recv.at[d], me_g, to)

    def rs_start(d):
        to, copy = chunk_out(d)

        @pl.when(to < n_early)
        def _():
            copy.start()

    def rs_start_late(d):
        to, copy = chunk_out(d)

        @pl.when(to >= n_early)
        def _():
            copy.start()

    def add_up(buf, count):
        total = buf[0]
        for i in range(1, count):
            total += buf[i]
        return total

    def across(d):
        own = ar_buf.at[me_g]
        return remote(own, own, ar_send.at[d], ar_recv.at[d], lax.rem(me_g + d, n_grp), me_b)

    def cluster_sum():
        rs_buf[me_b] = partial[pl.ds(pl.multiple_of(me_b * 8, 8), 8)]
        each(n_blk, lambda d: chunk_out(d)[1].wait_recv())
        ar_buf[me_g] = add_up(rs_buf, n_blk)
        each(n_grp, lambda d: across(d).start())

    def rows_of(b):
        return gram_ref.at[pl.ds(pl.multiple_of(b * 8, 8), 8)]

    def chunk_back(d, who):
        return remote(
            rows_of(who), rows_of(who), ag_send.at[d], ag_recv.at[d], me_g, lax.rem(me_b + d, n_blk)
        )

    def whole_sum():
        each(n_grp, lambda d: across(d).wait())
        gram_ref[pl.ds(pl.multiple_of(me_b * 8, 8), 8)] = add_up(ar_buf, n_grp)
        each(n_blk, lambda d: chunk_back(d, me_b).start())

    each(n_blk, rs_start)

    for d in range(1, side):
        for copy in p_second(d):
            copy.wait()
    pick(crossed(p_panel), p_out)
    p_across = exchange(p_out, p_in, 2)
    start(p_across)
    pass_on(s_panel, s_send, s_recv)
    sums = mix_inner(crossed(p_panel))
    wait(p_across)
    u = jnp.concatenate(mix_outer(sums, p_in), axis=1)
    partial[3 * k :, 0 : 3 * k] = dot_nt(u, basis, HIGH)
    each(n_blk, rs_start_late)

    @pl.when(me_b < n_early)
    def _():
        cluster_sum()

    all_in(s_panel, s_send, s_recv)
    pick(crossed(s_panel), s_out)
    s_across = exchange(s_out, s_in, 4)
    start(s_across)
    sums = mix_inner(crossed(s_panel))
    wait(s_across)
    t = jnp.concatenate(mix_outer(sums, s_in), axis=1)
    mine_t[:, 0 : 3 * k] = dot_nt(t, basis, HIGH)
    mine_t[:, 3 * k :] = jnp.zeros((k, k), F32)

    def half_of(ref, c):
        return ref.at[pl.ds(pl.multiple_of(c * half, 8), half)]

    to_mate = remote(half_of(mine_t, 1 - core), mate_t, mate_send.at[0], mate_recv.at[0], mate, me_b)
    to_mate.start()

    @pl.when(me_b >= n_early)
    def _():
        cluster_sum()

    to_mate.wait()
    blk_t[me_b] = mine_t[pl.ds(pl.multiple_of(core * half, 8), half)] + mate_t[...]

    def t_blk(d):
        own = blk_t.at[me_b]
        return remote(own, own, blk_send.at[d], blk_recv.at[d], me_g, lax.rem(me_b + d, n_blk))

    each(n_blk, lambda d: t_blk(d).start())

    @pl.when(me_b < n_early)
    def _():
        whole_sum()

    each(n_blk, lambda d: t_blk(d).wait())
    z_t[me_g // 2] = add_up(blk_t, n_blk)

    def t_z(d):
        own = z_t.at[me_g // 2]
        return remote(own, own, zt_send.at[d], zt_recv.at[d], lax.rem(me_g + 2 * d, n_grp), me_b)

    each(n_grp // 2, lambda d: t_z(d).start())

    @pl.when(me_b >= n_early)
    def _():
        whole_sum()

    each(n_grp // 2, lambda d: t_z(d).wait())
    image_ref[pl.ds(pl.multiple_of(core * half, 8), half)] = add_up(z_t, n_grp // 2)
    own_half = half_of(image_ref, core)
    back = remote(own_half, own_half, mate_send.at[1], mate_recv.at[1], mate, me_b)
    back.start()
    each(n_blk, lambda d: chunk_back(d, lax.rem(me_b + n_blk - d, n_blk)).wait_recv())
    each(n_blk, lambda d: chunk_back(d, me_b).wait_send())
    each(n_blk, lambda d: chunk_out(d)[1].wait_send())
    back.wait()


def first_kernel(mesh, tiles, cols, scales, x, p):
    n_grp, n_blk = mesh.shape["grp"], mesh.shape["blk"]
    side = 4
    k, here = x.shape
    rows_here, slots, width, _ = tiles.shape
    outer = rows_here * (slots // 8)
    vmem = pl.BlockSpec(memory_space=pltpu.VMEM)
    hbm = pl.BlockSpec(memory_space=pl.ANY)
    dma = pltpu.SemaphoreType.DMA
    across = pltpu.VMEM((2, outer, k, width), BF16)
    panel = pltpu.VMEM((rows_here, side, side, k, width), BF16)
    return pl.pallas_call(
        functools.partial(collect, n_grp, n_blk, side),
        out_shape=(
            jax.ShapeDtypeStruct((4 * k, 4 * k), F32),
            jax.ShapeDtypeStruct((k, 4 * k), F32),
            jax.ShapeDtypeStruct((k, here), F32),
        ),
        in_specs=[hbm] * 5,
        out_specs=(vmem, vmem, vmem),
        scratch_shapes=[
            pltpu.SMEM(cols.shape, jnp.int32),
            pltpu.SMEM(cols.shape, F32),
            pltpu.VMEM(x.shape, F32),
            pltpu.VMEM(x.shape, F32),
            pltpu.VMEM(tiles.shape, BF16),
            panel,
            panel,
            panel,
            pltpu.SMEM(cols.shape, jnp.int32),
            pltpu.SMEM(cols.shape, jnp.int32),
            across,
            across,
            across,
            across,
            across,
            across,
            pltpu.VMEM((4 * k, 4 * k), F32),
            pltpu.VMEM((n_blk, 8, 4 * k), F32),
            pltpu.VMEM((n_grp, 8, 4 * k), F32),
            pltpu.VMEM((k, 4 * k), F32),
            pltpu.VMEM((k // 2, 4 * k), F32),
            pltpu.VMEM((n_blk, k // 2, 4 * k), F32),
            pltpu.VMEM((n_grp // 2, k // 2, 4 * k), F32),
            dma((4 + rows_here,)),
            dma((2,)),
            dma((2,)),
            dma((2, side + 1, side)),
            dma((2, side + 1, side)),
            dma((2, side)),
            dma((2, side)),
            dma((2, side)),
            dma((2, side)),
            dma((2, side + 1, side)),
            dma((2, side + 1, side)),
            dma((6,)),
            dma((6,)),
            dma((n_blk,)),
            dma((n_blk,)),
            dma((n_grp,)),
            dma((n_grp,)),
            dma((n_blk,)),
            dma((n_blk,)),
            dma((2,)),
            dma((2,)),
            dma((n_blk,)),
            dma((n_blk,)),
            dma((n_grp // 2,)),
            dma((n_grp // 2,)),
        ],
        compiler_params=pltpu.CompilerParams(
            collective_id=0, has_side_effects=True, vmem_limit_bytes=56 * 2**20
        ),
        name="spread_and_mix",
    )(cols, scales, x, p, tiles)


def column(a, j, lanes):
    return jnp.broadcast_to(a[:, j : j + 1], (a.shape[0], lanes))


def spread_row(a, r):
    return jnp.broadcast_to(a[r : r + 1], a.shape)


def combine(
    inv_count, gram_ref, image_ref, s_ref, x_hbm, p_hbm, xn_ref, pn_ref, x_ref, p_ref, load_sem
):
    load = [
        pltpu.make_async_copy(x_hbm, x_ref, load_sem.at[0]),
        pltpu.make_async_copy(p_hbm, p_ref, load_sem.at[1]),
    ]
    for copy in load:
        copy.start()
    k = x_ref.shape[0]
    n = 3 * k
    gram = gram_ref[...] * inv_count
    on_t = (image_ref[...] * inv_count)[:, :n]
    basis = gram[:n, :n]
    raw = jnp.concatenate([basis[:, k : 2 * k], on_t.T, gram[n:, :n].T], axis=1)
    images = 0.5 * (raw + raw.T)

    groups = n // 8
    left = [basis[8 * q : 8 * q + 8] for q in range(groups)]
    right = [images[8 * q : 8 * q + 8] for q in range(groups)]
    pivots = [None] * groups
    coupling = None
    sub = lax.broadcasted_iota(jnp.int32, (8, n), 0)
    for start in range(0, n, PANEL):
        panel = [
            [column(left[g], start + c, n) for g in range(groups)] for c in range(PANEL)
        ]
        for c in range(PANEL):
            j = start + c
            q, r = j // 8, j % 8
            inv = 1.0 / spread_row(panel[c][q], r)
            pivots[q] = inv if r == 0 else jnp.where(sub == r, inv, pivots[q])
            here = [
                jnp.where(sub == r, 0.0, panel[c][g]) if g == q else panel[c][g]
                for g in range(groups)
            ]
            for later in range(c + 1, PANEL):
                factor = spread_row(panel[later][q], r) * inv
                panel[later] = [panel[later][g] - here[g] * factor for g in range(groups)]
            row_left = spread_row(left[q], r) * inv
            row_right = spread_row(right[q], r) * inv
            left = [left[g] - here[g] * row_left for g in range(groups)]
            right = [right[g] - here[g] * row_right for g in range(groups)]
            if j == k - 1:
                coupling = jnp.concatenate(
                    [(left[g] * pivots[g])[:, k : 2 * k] for g in range(k // 8)], axis=0
                )
    operator = jnp.concatenate([right[g] * pivots[g] for g in range(groups)], axis=0)

    here = lax.broadcasted_iota(jnp.int32, (n, n), 0) == lax.broadcasted_iota(jnp.int32, (n, n), 1)
    shift = jnp.sum(jnp.where(here, operator, 0.0), keepdims=True) * (1.0 / n)
    centred = operator - jnp.where(here, jnp.broadcast_to(shift, (n, n)), 0.0)
    size = jnp.sum(centred * centred.T, keepdims=True)
    iterate = centred * jnp.broadcast_to(lax.rsqrt(size + 1e-6), (n, n))
    for _ in range(NS_STEPS - 1):
        iterate = 1.5 * iterate - 0.5 * dot_nn(iterate, dot_nn(iterate, iterate))
    first = iterate[:, :k]
    first = 1.5 * first - 0.5 * dot_nn(iterate, dot_nn(iterate, first))
    coefficients = 0.5 * (jnp.where(here[:, :k], 1.0, 0.0) + first)

    flat = coefficients.T
    gram_new = dot_nn(flat, dot_nn(basis, coefficients))
    both = jnp.concatenate([gram_new, flat], axis=1)
    lanes = both.shape[1]
    rows = [both[8 * q : 8 * q + 8] for q in range(k // 8)]
    sub = lax.broadcasted_iota(jnp.int32, (8, lanes), 0)
    scale = [None] * (k // 8)
    for start in range(0, k, PANEL):
        first = start // 8
        below = range(first, k // 8)
        panel = [{g: column(rows[g], start + c, lanes) for g in below} for c in range(PANEL)]
        for c in range(PANEL):
            q, r = (start + c) // 8, (start + c) % 8
            pivot = spread_row(panel[c][q], r)
            inv = 1.0 / pivot
            root = lax.rsqrt(pivot)
            scale[q] = root if r == 0 else jnp.where(sub == r, root, scale[q])
            here = {
                g: jnp.where(sub <= r, 0.0, panel[c][g]) if g == q else panel[c][g] for g in below
            }
            for later in range(c + 1, PANEL):
                factor = spread_row(panel[later][q], r) * inv
                panel[later] = {g: panel[later][g] - here[g] * factor for g in below}
            row = spread_row(rows[q], r) * inv
            for g in below:
                rows[g] = rows[g] - here[g] * row
    solved = jnp.concatenate([rows[g] * scale[g] for g in range(k // 8)], axis=0)[:, k:]

    on_residual = solved[:, k : 2 * k]
    back = dot_nt(on_residual, coupling, HIGH)
    weights = jnp.concatenate(
        [solved, jnp.concatenate([-back, solved[:, k:]], axis=1)], axis=0
    )
    for copy in load:
        copy.wait()
    out = (
        dot_nn(weights[:, :k], x_ref[...])
        + dot_nn(weights[:, k : 2 * k], s_ref[...])
        + dot_nn(weights[:, 2 * k :], p_ref[...])
    )
    xn_ref[...] = out[:k]
    pn_ref[...] = out[k:]


def second_kernel(items, gram, image, s, x, p):
    vmem = pl.BlockSpec(memory_space=pltpu.VMEM)
    hbm = pl.BlockSpec(memory_space=pl.ANY)
    return pl.pallas_call(
        functools.partial(combine, 1.0 / items),
        out_shape=(
            jax.ShapeDtypeStruct(x.shape, F32),
            jax.ShapeDtypeStruct(p.shape, F32),
        ),
        in_specs=[vmem, vmem, vmem, hbm, hbm],
        out_specs=(vmem, vmem),
        scratch_shapes=[
            pltpu.VMEM(x.shape, F32),
            pltpu.VMEM(p.shape, F32),
            pltpu.SemaphoreType.DMA((2,)),
        ],
        compiler_params=pltpu.CompilerParams(vmem_limit_bytes=56 * 2**20),
        name="rayleigh_ritz",
    )(gram, image, s, x, p)


def solution(mesh):
    def per_device(tiles, cols, scales, x, p):
        items = x.shape[1] * mesh.shape["grp"] * mesh.shape["blk"]
        gram, image, s = first_kernel(mesh, tiles, cols, scales, x, p)
        return second_kernel(items, gram, image, s, x, p)

    placed = (
        P(("grp", "blk"), None, None, None),
        P(("grp", "blk"), None),
        P(("grp", "blk"), None),
        P(None, ("grp", "blk")),
        P(None, ("grp", "blk")),
    )
    return jax.shard_map(
        per_device,
        mesh=mesh,
        in_specs=placed,
        out_specs=(P(None, ("grp", "blk")), P(None, ("grp", "blk"))),
        check_vma=False,
    )
```

time: 579 us -> 68.1 us (0.12)
  waiting for transfers between devices: 311 us -> 0 us
  blocking collectives: 170 us -> 0 us
  Pallas kernels: 0 us -> 67.2 us
  other arithmetic: 36.5 us -> 0 us
  matrix products: 30.4 us -> 0 us
  between operations: 15.7 us -> 0.64 us
  starting transfers between devices: 9.49 us -> 0 us
    psum x1 -> x0, waiting for transfers between devices: 240 us -> none  [per_device(): lax.psum((jnp.dot(full_basis, full_basis.T, precision=high), jnp.dot(full...]
    psum x2 -> x0, blocking collectives: 152 us -> none  [the longest x1 77.5 us: per_device(): lax.psum((jnp.dot(x_start, x_start.T, precision=high), jnp.dot(x_start, i...]
    pallas_call x0 -> x2, Pallas kernels: none -> 67.2 us  [the longest x1 56.6 us: first_kernel(): pl.pallas_call(functools.partial(collect, n_grp, n_blk, side), out_shape=...]
    all_gather x1 -> x0, waiting for transfers between devices: 52.2 us -> none  [fetch_picked(): own_panel = lax.all_gather(rounded, 'blk', axis=1, tiled=True)]
    another operation x16 -> x0, other arithmetic: 30.8 us -> none  [the longest x6 14.2 us: lower_solve(): lax.linalg.triangular_solve(factor, rhs, left_side=True, lower=True, tran...]
    dot_general x28 -> x0, matrix products: 26.7 us -> none  [the longest x2 12.6 us: apply_local(): lax.dot_general(picked, block_tiles, (((3,), (3,)), ((1, 2), (0, 1))), pr...]
    ppermute x4 -> x0, waiting for transfers between devices: 18.8 us -> none  [passed_along(): lax.ppermute(shard, axis, [(i, (i + by) % size) for i in range(size)])]
    all_gather x1 -> x0, blocking collectives: 18.1 us -> none  [fetch_picked(): own_panel = lax.all_gather(rounded, 'blk', axis=1, tiled=True)]
  transfers between devices with their start and end apart: 6 -> 0, of which waited for: 6 -> 0; matrix products, arithmetic and copies ran while one was open for 0% -> 0% of each run, Pallas kernels for 0% -> 0%
where the time goes in v1:
time: 68.1 us; the launch traced here: 67.9 us
  Pallas kernels  67.2 us (99%)
    pallas_call x1, Pallas kernels, first_kernel(): pl.pallas_call(functools.partial(collect, n_grp, n_blk, side), out_shape=...  56.6 us
    pallas_call x1, Pallas kernels, second_kernel(): pl.pallas_call(functools.partial(combine, 1.0 / items), out_shape=(jax.Sh...  10.6 us

profile of v1, /device:TPU:1, one launch (start us, length us, event | category | flops | bytes accessed | tf_op | source)
XLA Modules:
  0.0 67.9 jit_solution(12855232899759387910)
XLA Ops:
  0.6 56.6 %spread_and_mix.1 = (f32[128,128]{1,0:T(8,128)}, f32[32,128]{1,0:T(8,128)}, f32[32,512]{1,0:T(8,128)}) custom-call(s32[2,32]{1,0:T(2,128)} %cols_hbm.1, f32[2,32]{1,0:T(2,128)} %scales_hbm.1, f32[32,512]{1,0:T(8,128)} %x_hbm.3, f32[32,512]{1,0:T(8,128)} %p_hbm.3, bf16[2,32,256,256]{3,2,1,0:T(8,128)(2,1)} %tiles_hbm.1), custom_call_target="tpu_custom_call" | custom-call | tf_op jit(solution)/shard_map/spread_and_mix/pallas_call | solution.py:439
  57.2 10.6 %rayleigh_ritz.1 = (f32[32,512]{1,0:T(8,128)}, f32[32,512]{1,0:T(8,128)}) custom-call(f32[128,128]{1,0:T(8,128)} %get-tuple-element.5.gram_ref, f32[32,128]{1,0:T(8,128)} %get-tuple-element.6.image_ref, f32[32,512]{1,0:T(8,128)} %get-tuple-element.7.s_ref, f32[32,512]{1,0:T(8,128)} %x_hbm.3, f32[32,512]{1,0:T(8,128)} %p_hbm.3), custom_call_target="tpu_custom_call" | custom-call | tf_op jit(solution)/shard_map/rayleigh_ritz/pallas_call | solution.py:620

commit v2 on v1

--- a/solution.py
+++ b/solution.py
@@ -24,10 +24,53 @@
     return jnp.dot(a, b, precision=precision, preferred_element_type=F32)
 
 
+def column(a, j, lanes):
+    return jnp.broadcast_to(a[:, j : j + 1], (a.shape[0], lanes))
+
+
+def spread_row(a, r):
+    return jnp.broadcast_to(a[r : r + 1], a.shape)
+
+
+def invert(gram, k):
+    n, lanes = gram.shape[0], 128
+    groups = n // PANEL
+    sub = lax.broadcasted_iota(jnp.int32, (PANEL, lanes), 0)
+    lane = lax.broadcasted_iota(jnp.int32, (PANEL, lanes), 1)
+    left = [gram[PANEL * g : PANEL * g + PANEL] for g in range(groups)]
+    right = [jnp.where(lane == sub + PANEL * g, 1.0, 0.0) for g in range(groups)]
+
+    def turn(_, both):
+        left, right = list(both[:groups]), list(both[groups:])
+        panel = [[column(left[g], c, lanes) for g in range(groups)] for c in range(PANEL)]
+        pivots = None
+        for c in range(PANEL):
+            inv = 1.0 / spread_row(panel[c][0], c)
+            pivots = inv if c == 0 else jnp.where(sub == c, inv, pivots)
+            here = [jnp.where(sub == c, 0.0, panel[c][0]), *panel[c][1:]]
+            for later in range(c + 1, PANEL):
+                factor = spread_row(panel[later][0], c) * inv
+                panel[later] = [panel[later][g] - here[g] * factor for g in range(groups)]
+            row_left = spread_row(left[0], c) * inv
+            row_right = spread_row(right[0], c) * inv
+            left = [left[g] - here[g] * row_left for g in range(groups)]
+            right = [right[g] - here[g] * row_right for g in range(groups)]
+        left[0], right[0] = left[0] * pivots, right[0] * pivots
+        left = [pltpu.roll(a, lanes - PANEL, 1) for a in left]
+        return (*left[1:], left[0], *right[1:], right[0])
+
+    turns = k // PANEL
+    both = lax.fori_loop(0, turns, turn, (*left, *right))
+    coupling = jnp.concatenate(both[groups - turns : groups], axis=0)[:, :k]
+    both = lax.fori_loop(turns, groups, turn, both)
+    return jnp.concatenate(both[groups:], axis=0), coupling
+
+
 def collect(
     n_grp,
     n_blk,
     side,
+    inv_count,
     cols_hbm,
     scales_hbm,
     x_hbm,
@@ -35,6 +78,8 @@
     tiles_hbm,
     gram_ref,
     image_ref,
+    inverse_ref,
+    coupling_ref,
     s_ref,
     cols,
     scales,
@@ -107,9 +152,7 @@
     load_x, load_p = load(x_hbm, x_ref, 0), load(p_hbm, p_ref, 1)
     load_small = [load(cols_hbm, cols, 2), load(scales_hbm, scales, 3)]
     load_tiles = [load(tiles_hbm.at[i], tiles.at[i], 4 + i) for i in range(rows_here)]
-    for copy in [load_x, load_p, *load_small, *load_tiles]:
-        copy.start()
-
+    load_x.start()
     barrier = pltpu.get_barrier_semaphore()
 
     def greet(grp, blk):
@@ -127,6 +170,8 @@
 
     lax.fori_loop(1, n_blk, greet_blk, 0)
     lax.fori_loop(1, n_grp, greet_grp, 0)
+    for copy in [*load_small, load_p, *load_tiles]:
+        copy.start()
 
     def block(ref, i):
         return ref[:, i * width : (i + 1) * width].astype(BF16)
@@ -134,11 +179,6 @@
     load_x.wait()
     for i in range(rows_here):
         x_panel[i, me_x, me_y] = block(x_ref, i)
-    load_p.wait()
-    for i in range(rows_here):
-        p_panel[i, me_x, me_y] = block(p_ref, i)
-    for copy in load_small:
-        copy.wait()
     pl.semaphore_wait(barrier, n_blk - 1 + n_grp - 1)
 
     def remote(src, dst, send, recv, grp, blk):
@@ -265,10 +305,16 @@
                 sums[i] += dot_nt(into[1, i * outer + j], tiles[i, b]) * scales[i, b]
         return sums
 
-    for copy in ask:
-        copy.start()
     send_own(x_panel, x_send, x_recv)
+    wait(load_small)
+    start(ask)
+    load_p.wait()
+    for i in range(rows_here):
+        p_panel[i, me_x, me_y] = block(p_ref, i)
     pass_on(x_panel, x_send, x_recv)
+    for d in range(1, side):
+        for copy in p_first(d):
+            copy.start()
     for copy in ask:
         copy.wait()
     all_in(x_panel, x_send, x_recv)
@@ -278,16 +324,13 @@
         copy.start()
     for d in range(1, side):
         for copy in p_first(d):
+            copy.wait()
+    for d in range(1, side):
+        for copy in p_second(d):
             copy.start()
     for copy in load_tiles:
         copy.wait()
     sums = mix_inner(crossed(x_panel))
-    for d in range(1, side):
-        for copy in p_first(d):
-            copy.wait()
-    for d in range(1, side):
-        for copy in p_second(d):
-            copy.start()
     for copy in x_across:
         copy.wait()
     sums = mix_outer(sums, x_in)
@@ -363,15 +406,15 @@
     u = jnp.concatenate(mix_outer(sums, p_in), axis=1)
     partial[3 * k :, 0 : 3 * k] = dot_nt(u, basis, HIGH)
     each(n_blk, rs_start_late)
-
-    @pl.when(me_b < n_early)
-    def _():
-        cluster_sum()
-
     all_in(s_panel, s_send, s_recv)
     pick(crossed(s_panel), s_out)
     s_across = exchange(s_out, s_in, 4)
     start(s_across)
+
+    @pl.when(me_b < n_early)
+    def _():
+        cluster_sum()
+
     sums = mix_inner(crossed(s_panel))
     wait(s_across)
     t = jnp.concatenate(mix_outer(sums, s_in), axis=1)
@@ -401,6 +444,16 @@
     def _():
         whole_sum()
 
+    def back_from(early):
+        def arrived(d):
+            source = lax.rem(me_b + n_blk - d, n_blk)
+
+            @pl.when((source < n_early) if early else (source >= n_early))
+            def _():
+                chunk_back(d, source).wait_recv()
+
+        return arrived
+
     each(n_blk, lambda d: t_blk(d).wait())
     z_t[me_g // 2] = add_up(blk_t, n_blk)
 
@@ -414,18 +467,22 @@
     def _():
         whole_sum()
 
+    each(n_blk, back_from(True))
+    inverse, coupling = invert(gram_ref[0 : 3 * k] * inv_count, k)
+    inverse_ref[...] = inverse
+    coupling_ref[...] = coupling
     each(n_grp // 2, lambda d: t_z(d).wait())
     image_ref[pl.ds(pl.multiple_of(core * half, 8), half)] = add_up(z_t, n_grp // 2)
     own_half = half_of(image_ref, core)
     back = remote(own_half, own_half, mate_send.at[1], mate_recv.at[1], mate, me_b)
     back.start()
-    each(n_blk, lambda d: chunk_back(d, lax.rem(me_b + n_blk - d, n_blk)).wait_recv())
+    each(n_blk, back_from(False))
     each(n_blk, lambda d: chunk_back(d, me_b).wait_send())
     each(n_blk, lambda d: chunk_out(d)[1].wait_send())
     back.wait()
 
 
-def first_kernel(mesh, tiles, cols, scales, x, p):
+def first_kernel(mesh, items, tiles, cols, scales, x, p):
     n_grp, n_blk = mesh.shape["grp"], mesh.shape["blk"]
     side = 4
     k, here = x.shape
@@ -437,14 +494,16 @@
     across = pltpu.VMEM((2, outer, k, width), BF16)
     panel = pltpu.VMEM((rows_here, side, side, k, width), BF16)
     return pl.pallas_call(
-        functools.partial(collect, n_grp, n_blk, side),
+        functools.partial(collect, n_grp, n_blk, side, 1.0 / items),
         out_shape=(
             jax.ShapeDtypeStruct((4 * k, 4 * k), F32),
             jax.ShapeDtypeStruct((k, 4 * k), F32),
+            jax.ShapeDtypeStruct((3 * k, 4 * k), F32),
+            jax.ShapeDtypeStruct((k, k), F32),
             jax.ShapeDtypeStruct((k, here), F32),
         ),
         in_specs=[hbm] * 5,
-        out_specs=(vmem, vmem, vmem),
+        out_specs=(vmem,) * 5,
         scratch_shapes=[
             pltpu.SMEM(cols.shape, jnp.int32),
             pltpu.SMEM(cols.shape, F32),
@@ -502,62 +561,36 @@
     )(cols, scales, x, p, tiles)
 
 
-def column(a, j, lanes):
-    return jnp.broadcast_to(a[:, j : j + 1], (a.shape[0], lanes))
-
-
-def spread_row(a, r):
-    return jnp.broadcast_to(a[r : r + 1], a.shape)
-
-
 def combine(
-    inv_count, gram_ref, image_ref, s_ref, x_hbm, p_hbm, xn_ref, pn_ref, x_ref, p_ref, load_sem
+    inv_count,
+    gram_ref,
+    image_ref,
+    inverse_ref,
+    coupling_ref,
+    s_ref,
+    x_hbm,
+    p_hbm,
+    xn_ref,
+    pn_ref,
+    rows_ref,
+    load_sem,
 ):
+    k = s_ref.shape[0]
+    n = 3 * k
     load = [
-        pltpu.make_async_copy(x_hbm, x_ref, load_sem.at[0]),
-        pltpu.make_async_copy(p_hbm, p_ref, load_sem.at[1]),
+        pltpu.make_async_copy(x_hbm, rows_ref.at[0:k], load_sem.at[0]),
+        pltpu.make_async_copy(p_hbm, rows_ref.at[2 * k : n], load_sem.at[1]),
     ]
     for copy in load:
         copy.start()
-    k = x_ref.shape[0]
-    n = 3 * k
+    rows_ref[k : 2 * k] = s_ref[...]
     gram = gram_ref[...] * inv_count
     on_t = (image_ref[...] * inv_count)[:, :n]
     basis = gram[:n, :n]
     raw = jnp.concatenate([basis[:, k : 2 * k], on_t.T, gram[n:, :n].T], axis=1)
     images = 0.5 * (raw + raw.T)
 
-    groups = n // 8
-    left = [basis[8 * q : 8 * q + 8] for q in range(groups)]
-    right = [images[8 * q : 8 * q + 8] for q in range(groups)]
-    pivots = [None] * groups
-    coupling = None
-    sub = lax.broadcasted_iota(jnp.int32, (8, n), 0)
-    for start in range(0, n, PANEL):
-        panel = [
-            [column(left[g], start + c, n) for g in range(groups)] for c in range(PANEL)
-        ]
-        for c in range(PANEL):
-            j = start + c
-            q, r = j // 8, j % 8
-            inv = 1.0 / spread_row(panel[c][q], r)
-            pivots[q] = inv if r == 0 else jnp.where(sub == r, inv, pivots[q])
-            here = [
-                jnp.where(sub == r, 0.0, panel[c][g]) if g == q else panel[c][g]
-                for g in range(groups)
-            ]
-            for later in range(c + 1, PANEL):
-                factor = spread_row(panel[later][q], r) * inv
-                panel[later] = [panel[later][g] - here[g] * factor for g in range(groups)]
-            row_left = spread_row(left[q], r) * inv
-            row_right = spread_row(right[q], r) * inv
-            left = [left[g] - here[g] * row_left for g in range(groups)]
-            right = [right[g] - here[g] * row_right for g in range(groups)]
-            if j == k - 1:
-                coupling = jnp.concatenate(
-                    [(left[g] * pivots[g])[:, k : 2 * k] for g in range(k // 8)], axis=0
-                )
-    operator = jnp.concatenate([right[g] * pivots[g] for g in range(groups)], axis=0)
+    operator = dot_nn(inverse_ref[:, :n], images)
 
     here = lax.broadcasted_iota(jnp.int32, (n, n), 0) == lax.broadcasted_iota(jnp.int32, (n, n), 1)
     shift = jnp.sum(jnp.where(here, operator, 0.0), keepdims=True) * (1.0 / n)
@@ -599,22 +632,18 @@
     solved = jnp.concatenate([rows[g] * scale[g] for g in range(k // 8)], axis=0)[:, k:]
 
     on_residual = solved[:, k : 2 * k]
-    back = dot_nt(on_residual, coupling, HIGH)
+    back = dot_nt(on_residual, coupling_ref[...], HIGH)
     weights = jnp.concatenate(
         [solved, jnp.concatenate([-back, solved[:, k:]], axis=1)], axis=0
     )
     for copy in load:
         copy.wait()
-    out = (
-        dot_nn(weights[:, :k], x_ref[...])
-        + dot_nn(weights[:, k : 2 * k], s_ref[...])
-        + dot_nn(weights[:, 2 * k :], p_ref[...])
-    )
+    out = dot_nn(weights, rows_ref[...])
     xn_ref[...] = out[:k]
     pn_ref[...] = out[k:]
 
 
-def second_kernel(items, gram, image, s, x, p):
+def second_kernel(items, gram, image, inverse, coupling, s, x, p):
     vmem = pl.BlockSpec(memory_space=pltpu.VMEM)
     hbm = pl.BlockSpec(memory_space=pl.ANY)
     return pl.pallas_call(
@@ -623,23 +652,22 @@
             jax.ShapeDtypeStruct(x.shape, F32),
             jax.ShapeDtypeStruct(p.shape, F32),
         ),
-        in_specs=[vmem, vmem, vmem, hbm, hbm],
+        in_specs=[vmem] * 5 + [hbm] * 2,
         out_specs=(vmem, vmem),
         scratch_shapes=[
-            pltpu.VMEM(x.shape, F32),
-            pltpu.VMEM(p.shape, F32),
+            pltpu.VMEM((3 * x.shape[0], x.shape[1]), F32),
             pltpu.SemaphoreType.DMA((2,)),
         ],
         compiler_params=pltpu.CompilerParams(vmem_limit_bytes=56 * 2**20),
         name="rayleigh_ritz",
-    )(gram, image, s, x, p)
+    )(gram, image, inverse, coupling, s, x, p)
 
 
 def solution(mesh):
     def per_device(tiles, cols, scales, x, p):
         items = x.shape[1] * mesh.shape["grp"] * mesh.shape["blk"]
-        gram, image, s = first_kernel(mesh, tiles, cols, scales, x, p)
-        return second_kernel(items, gram, image, s, x, p)
+        sums = first_kernel(mesh, items, tiles, cols, scales, x, p)
+        return second_kernel(items, *sums, x, p)
 
     placed = (
         P(("grp", "blk"), None, None, None),

time: 68.1 us -> 62.3 us (0.915)
  Pallas kernels: 67.2 us -> 61.4 us
    pallas_call x1, Pallas kernels: 56.6 us -> 53.6 us  [first_kernel(): pl.pallas_call(functools.partial(collect, n_grp, n_blk, side, 1.0 / items...]
    pallas_call x1, Pallas kernels: 10.6 us -> 7.82 us  [second_kernel(): pl.pallas_call(functools.partial(combine, 1.0 / items), out_shape=(jax.Sh...]
where the time goes in v2:
time: 62.3 us; the launch traced here: 62.1 us
  Pallas kernels  61.4 us (99%)
  between operations  0.64 us (1%)
    pallas_call x1, Pallas kernels, first_kernel(): pl.pallas_call(functools.partial(collect, n_grp, n_blk, side, 1.0 / items...  53.6 us
    pallas_call x1, Pallas kernels, second_kernel(): pl.pallas_call(functools.partial(combine, 1.0 / items), out_shape=(jax.Sh...  7.82 us

profile of v2, /device:TPU:1, one launch (start us, length us, event | category | flops | bytes accessed | tf_op | source)
XLA Modules:
  0.0 62.1 jit_solution(6067934446883644334)
XLA Ops:
  0.6 53.6 %spread_and_mix.1 = (f32[128,128]{1,0:T(8,128)}, f32[32,128]{1,0:T(8,128)}, f32[96,128]{1,0:T(8,128)}, f32[32,32]{1,0:T(8,128)}, f32[32,512]{1,0:T(8,128)}) custom-call(s32[2,32]{1,0:T(2,128)} %cols_hbm.1, f32[2,32]{1,0:T(2,128)} %scales_hbm.1, f32[32,512]{1,0:T(8,128)} %x_hbm.3, f32[32,512]{1,0:T(8,128)} %p_hbm.3, bf16[2,32,256,256]{3,2,1,0:T(8,128)(2,1)} %tiles_hbm.1), custom_call_target="tpu_custom_call" | custom-call | tf_op jit(solution)/shard_map/spread_and_mix/pallas_call | solution.py:496
  54.2 7.8 %rayleigh_ritz.1 = (f32[32,512]{1,0:T(8,128)}, f32[32,512]{1,0:T(8,128)}) custom-call(f32[128,128]{1,0:T(8,128)} %get-tuple-element.7.gram_ref, f32[32,128]{1,0:T(8,128)} %get-tuple-element.8.image_ref, f32[96,128]{1,0:T(8,128)} %get-tuple-element.9.inverse_ref, f32[32,32]{1,0:T(8,128)} %get-tuple-element.10.coupling_ref, ...), custom_call_target="tpu_custom_call" | custom-call | tf_op jit(solution)/shard_map/rayleigh_ritz/pallas_call | solution.py:649

commit v3 on v2

--- a/solution.py
+++ b/solution.py
@@ -89,8 +89,7 @@
     x_panel,
     p_panel,
     s_panel,
-    want_next,
-    want_prev,
+    wanted,
     x_out,
     x_in,
     p_out,
@@ -192,8 +191,8 @@
         )
 
     ask = [
-        remote(cols, want_next, ask_send.at[0], ask_recv.at[0], prv, me_b),
-        remote(cols, want_prev, ask_send.at[1], ask_recv.at[1], nxt, me_b),
+        remote(cols, wanted.at[0], ask_send.at[0], ask_recv.at[0], prv, me_b),
+        remote(cols, wanted.at[1], ask_send.at[1], ask_recv.at[1], nxt, me_b),
     ]
 
     def each(count, act):
@@ -275,17 +274,27 @@
 
         return get
 
-    def exchange(out, into, at):
-        return [
-            remote(out.at[0], into.at[0], z_send.at[at], z_recv.at[at], nxt, me_b),
-            remote(out.at[1], into.at[1], z_send.at[at + 1], z_recv.at[at + 1], prv, me_b),
-        ]
-
-    def pick(get, out):
-        for i in range(rows_here):
-            for j in range(outer):
-                out[0, i * outer + j] = get(want_next[i, inner + j])
-                out[1, i * outer + j] = get(want_prev[i, inner + outer + j])
+    away = 1 - core
+
+    def exchange(out, into, at, side):
+        return remote(
+            out.at[side],
+            into.at[side],
+            z_send.at[at + side],
+            z_recv.at[at + side],
+            jnp.where(side == 0, nxt, prv),
+            me_b,
+        )
+
+    def hand_over(get, out, into, at):
+        copies = [exchange(out, into, at, side) for side in (away, 1 - away)]
+        for side, copy in zip((away, 1 - away), copies):
+            for i in range(rows_here):
+                for j in range(outer):
+                    slot = inner + side * outer + j
+                    out[side, i * outer + j] = get(wanted[side, i, slot])
+            copy.start()
+        return copies
 
     def mix_inner(get):
         sums = []
@@ -294,7 +303,7 @@
             def body(j, acc, i=i):
                 return acc + dot_nt(get(cols[i, j]), tiles[i, j]) * scales[i, j]
 
-            sums.append(lax.fori_loop(0, inner, body, jnp.zeros((k, width), F32), unroll=8))
+            sums.append(lax.fori_loop(0, inner, body, jnp.zeros((k, width), F32), unroll=24))
         return sums
 
     def mix_outer(sums, into):
@@ -318,10 +327,7 @@
     for copy in ask:
         copy.wait()
     all_in(x_panel, x_send, x_recv)
-    pick(crossed(x_panel), x_out)
-    x_across = exchange(x_out, x_in, 0)
-    for copy in x_across:
-        copy.start()
+    x_across = hand_over(crossed(x_panel), x_out, x_in, 0)
     for d in range(1, side):
         for copy in p_first(d):
             copy.wait()
@@ -397,9 +403,7 @@
     for d in range(1, side):
         for copy in p_second(d):
             copy.wait()
-    pick(crossed(p_panel), p_out)
-    p_across = exchange(p_out, p_in, 2)
-    start(p_across)
+    p_across = hand_over(crossed(p_panel), p_out, p_in, 2)
     pass_on(s_panel, s_send, s_recv)
     sums = mix_inner(crossed(p_panel))
     wait(p_across)
@@ -407,9 +411,7 @@
     partial[3 * k :, 0 : 3 * k] = dot_nt(u, basis, HIGH)
     each(n_blk, rs_start_late)
     all_in(s_panel, s_send, s_recv)
-    pick(crossed(s_panel), s_out)
-    s_across = exchange(s_out, s_in, 4)
-    start(s_across)
+    s_across = hand_over(crossed(s_panel), s_out, s_in, 4)
 
     @pl.when(me_b < n_early)
     def _():
@@ -513,8 +515,7 @@
             panel,
             panel,
             panel,
-            pltpu.SMEM(cols.shape, jnp.int32),
-            pltpu.SMEM(cols.shape, jnp.int32),
+            pltpu.SMEM((2, *cols.shape), jnp.int32),
             across,
             across,
             across,
@@ -603,6 +604,9 @@
     first = 1.5 * first - 0.5 * dot_nn(iterate, dot_nn(iterate, first))
     coefficients = 0.5 * (jnp.where(here[:, :k], 1.0, 0.0) + first)
 
+    for copy in load:
+        copy.wait()
+    members = rows_ref[...]
     flat = coefficients.T
     gram_new = dot_nn(flat, dot_nn(basis, coefficients))
     both = jnp.concatenate([gram_new, flat], axis=1)
@@ -636,9 +640,7 @@
     weights = jnp.concatenate(
         [solved, jnp.concatenate([-back, solved[:, k:]], axis=1)], axis=0
     )
-    for copy in load:
-        copy.wait()
-    out = dot_nn(weights, rows_ref[...])
+    out = dot_nn(weights, members)
     xn_ref[...] = out[:k]
     pn_ref[...] = out[k:]
 

time: 62.3 us -> 61 us (0.979)
  Pallas kernels: 61.4 us -> 60.3 us
    pallas_call x1, Pallas kernels: 53.6 us -> 52.9 us  [first_kernel(): pl.pallas_call(functools.partial(collect, n_grp, n_blk, side, 1.0 / items...]
where the time goes in v3:
time: 61 us; the launch traced here: 60.9 us
  Pallas kernels  60.3 us (99%)
  between operations  0.64 us (1%)
    pallas_call x1, Pallas kernels, first_kernel(): pl.pallas_call(functools.partial(collect, n_grp, n_blk, side, 1.0 / items...  52.9 us
    pallas_call x1, Pallas kernels, second_kernel(): pl.pallas_call(functools.partial(combine, 1.0 / items), out_shape=(jax.Sh...  7.32 us

profile of v3, /device:TPU:1, one launch (start us, length us, event | category | flops | bytes accessed | tf_op | source)
XLA Modules:
  0.0 60.9 jit_solution(3932702770767315271)
XLA Ops:
  0.6 52.9 %spread_and_mix.1 = (f32[128,128]{1,0:T(8,128)}, f32[32,128]{1,0:T(8,128)}, f32[96,128]{1,0:T(8,128)}, f32[32,32]{1,0:T(8,128)}, f32[32,512]{1,0:T(8,128)}) custom-call(s32[2,32]{1,0:T(2,128)} %cols_hbm.1, f32[2,32]{1,0:T(2,128)} %scales_hbm.1, f32[32,512]{1,0:T(8,128)} %x_hbm.3, f32[32,512]{1,0:T(8,128)} %p_hbm.3, bf16[2,32,256,256]{3,2,1,0:T(8,128)(2,1)} %tiles_hbm.1), custom_call_target="tpu_custom_call" | custom-call | tf_op jit(solution)/shard_map/spread_and_mix/pallas_call | solution.py:498
  53.6 7.3 %rayleigh_ritz.1 = (f32[32,512]{1,0:T(8,128)}, f32[32,512]{1,0:T(8,128)}) custom-call(f32[128,128]{1,0:T(8,128)} %get-tuple-element.7.gram_ref, f32[32,128]{1,0:T(8,128)} %get-tuple-element.8.image_ref, f32[96,128]{1,0:T(8,128)} %get-tuple-element.9.inverse_ref, f32[32,32]{1,0:T(8,128)} %get-tuple-element.10.coupling_ref, ...), custom_call_target="tpu_custom_call" | custom-call | tf_op jit(solution)/shard_map/rayleigh_ritz/pallas_call | solution.py:651

commit v4 on v3

--- a/solution.py
+++ b/solution.py
@@ -249,6 +249,10 @@
         each(side, lambda d: start(near(buf, send, recv, d)))
         each(side, lambda d: start(onward(buf, send, recv, 0, d)))
 
+    def send_own_row(buf, send, recv, i):
+        each(side, lambda d: near(buf, send, recv, d)[i].start())
+        each(side, lambda d: onward(buf, send, recv, 0, d)[i].start())
+
     def pass_on(buf, send, recv):
         def arrived(e):
             for copy in near(buf, send, recv, e):
@@ -306,13 +310,15 @@
             sums.append(lax.fori_loop(0, inner, body, jnp.zeros((k, width), F32), unroll=24))
         return sums
 
+    def mix_outer_row(total, into, i):
+        for j in range(outer):
+            a, b = inner + j, inner + outer + j
+            total += dot_nt(into[0, i * outer + j], tiles[i, a]) * scales[i, a]
+            total += dot_nt(into[1, i * outer + j], tiles[i, b]) * scales[i, b]
+        return total
+
     def mix_outer(sums, into):
-        for i in range(rows_here):
-            for j in range(outer):
-                a, b = inner + j, inner + outer + j
-                sums[i] += dot_nt(into[0, i * outer + j], tiles[i, a]) * scales[i, a]
-                sums[i] += dot_nt(into[1, i * outer + j], tiles[i, b]) * scales[i, b]
-        return sums
+        return [mix_outer_row(sums[i], into, i) for i in range(rows_here)]
 
     send_own(x_panel, x_send, x_recv)
     wait(load_small)
@@ -339,11 +345,11 @@
     sums = mix_inner(crossed(x_panel))
     for copy in x_across:
         copy.wait()
-    sums = mix_outer(sums, x_in)
     for i in range(rows_here):
-        s_panel[i, me_x, me_y] = sums[i].astype(BF16)
-        s_ref[:, i * width : (i + 1) * width] = sums[i]
-    send_own(s_panel, s_send, s_recv)
+        total = mix_outer_row(sums[i], x_in, i)
+        s_panel[i, me_x, me_y] = total.astype(BF16)
+        send_own_row(s_panel, s_send, s_recv, i)
+        s_ref[:, i * width : (i + 1) * width] = total
 
     basis = jnp.concatenate([x_ref[...], s_ref[...], p_ref[...]], axis=0)
     partial[0 : 3 * k, 0 : 3 * k] = dot_nt(basis, basis, HIGH)

time: 61 us -> 61.2 us (level)
  no operation moved by 1% of the time
where the time goes in v4:
time: 61.2 us; the launch traced here: 61.1 us
  Pallas kernels  60.4 us (99%)
  between operations  0.64 us (1%)
    pallas_call x1, Pallas kernels, first_kernel(): pl.pallas_call(functools.partial(collect, n_grp, n_blk, side, 1.0 / items...  53.1 us
    pallas_call x1, Pallas kernels, second_kernel(): pl.pallas_call(functools.partial(combine, 1.0 / items), out_shape=(jax.Sh...  7.32 us

profile of v4, /device:TPU:1, one launch (start us, length us, event | category | flops | bytes accessed | tf_op | source)
XLA Modules:
  0.0 61.1 jit_solution(11293859325740832948)
XLA Ops:
  0.6 53.1 %spread_and_mix.1 = (f32[128,128]{1,0:T(8,128)}, f32[32,128]{1,0:T(8,128)}, f32[96,128]{1,0:T(8,128)}, f32[32,32]{1,0:T(8,128)}, f32[32,512]{1,0:T(8,128)}) custom-call(s32[2,32]{1,0:T(2,128)} %cols_hbm.1, f32[2,32]{1,0:T(2,128)} %scales_hbm.1, f32[32,512]{1,0:T(8,128)} %x_hbm.3, f32[32,512]{1,0:T(8,128)} %p_hbm.3, bf16[2,32,256,256]{3,2,1,0:T(8,128)(2,1)} %tiles_hbm.1), custom_call_target="tpu_custom_call" | custom-call | tf_op jit(solution)/shard_map/spread_and_mix/pallas_call | solution.py:504
  53.7 7.3 %rayleigh_ritz.1 = (f32[32,512]{1,0:T(8,128)}, f32[32,512]{1,0:T(8,128)}) custom-call(f32[128,128]{1,0:T(8,128)} %get-tuple-element.7.gram_ref, f32[32,128]{1,0:T(8,128)} %get-tuple-element.8.image_ref, f32[96,128]{1,0:T(8,128)} %get-tuple-element.9.inverse_ref, f32[32,32]{1,0:T(8,128)} %get-tuple-element.10.coupling_ref, ...), custom_call_target="tpu_custom_call" | custom-call | tf_op jit(solution)/shard_map/rayleigh_ritz/pallas_call | solution.py:657
